TPU v7x, 32 devices: a whole 2x2x4 slice. The times are simulated.
32 devices in a mesh: tower: 2 (over core), shard: 16 (over z, y, x).
Axes of the slice: x: 2, y: 2, z: 4, core: 2. Of those that a mesh axis runs over, the one named last changes fastest.
Arguments:
- hidden: bfloat16 [2, 8192, 4096], P('tower', 'shard'), may hold values from -6 to 6
- head: float32 [2, 4096, 512], P('tower'), may hold values from -0.09375 to 0.09375
- pos_local: int32 [8192], P('shard'), may hold values from 0 to 511
- requests: int32 [16, 16, 4], P(None, 'shard'), may hold values from 0 to 511, as said below
- neg_slot: int32 [8192, 8], P('shard'), may hold values from 0 to 63
Outputs:
- head_grad: float32 [2, 4096, 512], P('tower', 'shard')
Inputs may be any that keep to these rules, and one draw needn't show every extreme that they name: requests[s, o, :] names 4 different rows of owner o.
All inputs are finite; a program needn't handle non-finite values.
Results may differ from a plain program's by a relative error of at most 0.0004.
The roundings to bfloat16 on the way count: a program that leaves them out, or rounds other values in their place, can miss the bound.
Values may be sent and summed in bfloat16 or wider, within the bound.
A program may use at most 128 MiB of HBM per device.

v0:
```python
import jax
import jax.numpy as jnp
from jax import lax
from jax.sharding import PartitionSpec as P

logit_divisor = 0.05
epsilon = 1e-06


def passed_along(block, axis, distance):
    devices = range(lax.axis_size(axis))
    route = [(i - distance, i) for i in devices if i - distance in devices]
    return lax.ppermute(block, axis, route)


def shards(hidden, head, pos_local, requests, neg_slot):
    hidden_rows = hidden[0]
    weights = head[0]
    row_count = hidden_rows.shape[0]
    shard_count = lax.axis_size("shard")
    slot_count = requests.shape[2]
    neg_count = neg_slot.shape[1]
    slot_total = shard_count * slot_count
    embedded = jnp.dot(
        hidden_rows, weights, precision=lax.Precision.HIGHEST, preferred_element_type=jnp.float32
    )
    magnitude = jnp.sqrt(jnp.sum(embedded * embedded, axis=1, keepdims=True) + epsilon)
    unit_rows = embedded / magnitude
    normalized_passages = unit_rows.astype(jnp.bfloat16)
    wanted_rows = requests[:, 0, :]
    sent_rows = lax.all_to_all(
        normalized_passages[wanted_rows], "shard", split_axis=0, concat_axis=0, tiled=True
    )
    joined_rows = jnp.concatenate([normalized_passages, sent_rows.reshape(slot_total, -1)], axis=0)
    arrived_rows = passed_along(joined_rows, "tower", -1)
    partner_vectors = arrived_rows[:row_count]
    pulled = arrived_rows[row_count:]
    mined_rows = pulled[neg_slot]
    cobatch_logits = (
        jnp.einsum(
            "ot,bt->ob", normalized_passages, partner_vectors, preferred_element_type=jnp.float32
        )
        / logit_divisor
    )
    distractor_logits = (
        jnp.einsum(
            "ip,ikp->ik", normalized_passages, mined_rows, preferred_element_type=jnp.float32
        )
        / logit_divisor
    )
    logits = jnp.concatenate([cobatch_logits, distractor_logits], axis=1)
    softmax_rows = jax.nn.softmax(logits, axis=1)
    columns = jnp.arange(row_count + neg_count, dtype=jnp.int32)[None, :]
    target = (pos_local[:, None] == columns).astype(jnp.float32)
    dlog = (softmax_rows - target).astype(jnp.bfloat16)
    cobatch_logit_adjoint = dlog[:, :row_count]
    distractor_logit_adjoint = dlog[:, row_count:]
    question_embedding_adjoint = (
        jnp.dot(cobatch_logit_adjoint, partner_vectors, preferred_element_type=jnp.float32)
        + jnp.einsum(
            "ik,ikp->ip", distractor_logit_adjoint, mined_rows, preferred_element_type=jnp.float32
        )
    ) / logit_divisor
    document_embedding_adjoint = (
        jnp.einsum(
            "en,er->nr",
            cobatch_logit_adjoint,
            normalized_passages,
            preferred_element_type=jnp.float32,
        )
        / logit_divisor
    )
    slot_ids = jnp.arange(slot_total, dtype=jnp.int32)[None, :]
    hardest_distractor_inputs = distractor_logit_adjoint.astype(jnp.float32)
    slot_weight = jnp.zeros((row_count, slot_total), jnp.float32)
    for column in range(neg_count):
        slot_weight = slot_weight + jnp.where(
            neg_slot[:, column : column + 1] == slot_ids,
            hardest_distractor_inputs[:, column : column + 1],
            0.0,
        )
    place_adjoint_lines = (
        jnp.dot(
            slot_weight.T, normalized_passages.astype(jnp.float32), precision=lax.Precision.HIGHEST
        )
        / logit_divisor
    )
    flat_wanted = wanted_rows.reshape(-1)
    row_ids = jnp.arange(row_count, dtype=jnp.int32)[:, None]
    owner_table = (row_ids == flat_wanted[None, :]).astype(jnp.float32)
    joined_grads = jnp.concatenate([document_embedding_adjoint, place_adjoint_lines], axis=0)
    arrived_grads = passed_along(joined_grads, "tower", 1)
    got_inbatch = arrived_grads[:row_count]
    got_slots = arrived_grads[row_count:].reshape(shard_count, slot_count, -1)
    returned_slots = lax.all_to_all(
        got_slots.astype(jnp.bfloat16), "shard", split_axis=0, concat_axis=0, tiled=True
    ).astype(got_slots.dtype)
    returned = got_inbatch + jnp.dot(
        owner_table, returned_slots.reshape(slot_total, -1), precision=lax.Precision.HIGHEST
    )
    is_query = lax.axis_index("tower") == 0
    d_unit = jnp.where(is_query, question_embedding_adjoint, returned)
    d_embedded = (
        d_unit - unit_rows * jnp.sum(unit_rows * d_unit, axis=1, keepdims=True)
    ) / magnitude
    head_grad = lax.psum_scatter(
        jnp.einsum(
            "rd,rp->dp",
            hidden_rows,
            d_embedded,
            precision=lax.Precision.HIGHEST,
            preferred_element_type=jnp.float32,
        ),
        "shard",
        scatter_dimension=0,
        tiled=True,
    )
    return head_grad[None]


def solution(mesh):
    placed = (
        P("tower", "shard", None),
        P("tower", None, None),
        P("shard"),
        P(None, "shard", None),
        P("shard", None),
    )
    return jax.shard_map(
        shards, mesh=mesh, in_specs=placed, out_specs=P("tower", "shard", None), check_vma=False
    )
```

profile of v0, /device:TPU:1, one launch (start us, length us, event | category | flops | bytes accessed | tf_op | source)
XLA Modules:
  0.0 279.5 jit_solution(7049308603471217378)
XLA Ops:
  6.5 0.7 compare_select_fusion.1
  7.4 11.3 %multiply_reduce_fusion.1 = (f32[512]{0:T(512)S(1)}, f32[512,512]{1,0:T(8,128)S(1)}) fusion(f32[1,4096,512]{2,1,0:T(8,128)} %param.6, bf16[1,512,4096]{2,1,0:T(8,128)(2,1)} %param.5), kind=kOutput, calls=%fused_computation.28 | convolution fusion | flops 12885426176 | bytes 13633536 | tf_op jit(solution)/shard_map/dot_general | solution.py:24
  18.9 0.7 gather_fusion
  19.6 0.7 reshape.54
  20.3 7.4 %all-to-all-start = ((bf16[16,4,512]{2,1,0:T(4,128)(2,1)}), bf16[16,4,512]{2,1,0:T(4,128)(2,1)S(1)}, u32[]{:S(2)}, u32[]{:S(2)}) async-start(bf16[16,4,512]{2,1,0:T(4,128)(2,1)} %reshape.54), calls=%async_computation | async-start | bytes 131072 | tf_op jit(solution)/shard_map/all_to_all | solution.py:31
  27.7 6.4 %all-to-all-done = bf16[16,4,512]{2,1,0:T(4,128)(2,1)S(1)} async-done(((bf16[16,4,512]{2,1,0:T(4,128)(2,1)}), bf16[16,4,512]{2,1,0:T(4,128)(2,1)S(1)}, u32[]{:S(2)}, u32[]{:S(2)}) %all-to-all-start) | async-done | bytes 65568 | tf_op jit(solution)/shard_map/all_to_all | solution.py:31
  34.1 4.0 %collective-permute-start = (bf16[576,512]{1,0:T(8,128)(2,1)S(1)}, bf16[576,512]{1,0:T(8,128)(2,1)S(1)}, u32[]{:S(2)}, u32[]{:S(2)}) collective-permute-start(bf16[576,512]{1,0:T(8,128)(2,1)S(1)} %pad_maximum_fusion.1), channel_id=1, source_target_pairs={{16,0},{17,1},{18,2},{19,3},{20,4},{21,5},{22,6},{23,7},{24,8},{25... | collective-permute-start | bytes 1769480 | tf_op jit(solution)/shard_map/ppermute | solution.py:13
  38.3 0.2 reshape.63
  38.7 1.1 collective-permute-done
  39.8 17.3 %gather_fusion.1 = bf16[4096,512]{1,0:T(8,128)(2,1)} fusion(bf16[64,512]{1,0:T(8,128)(2,1)S(1)} %slice.94, s32[4096]{0:T(1024)S(1)} %broadcast_clamp_fusion), kind=kCustom, calls=%fused_computation.1 | custom fusion | bytes 8404992 | tf_op jit(solution)/shard_map/gather | solution.py:38
  57.0 4.0 %fusion.2 = f32[512,1,8]{2,1,0:T(1,128)S(1)} fusion(bf16[4096,512]{1,0:T(8,128)(2,1)} %gather_fusion.1, bf16[512,512,1]{1,0,2:T(8,128)(2,1)S(1)} %fusion.66), kind=kOutput, calls=%fused_computation.5 | convolution fusion | flops 4194304 | bytes 4734976 | tf_op jit(solution)/shard_map/ip,ikp->ik/dot_general | solution.py:46
  61.1 0.2 fusion.58
  61.3 0.6 fusion.61
  61.8 0.4 fusion.15
  62.2 0.4 subtract_convert_fusion
  62.7 0.5 convolution_multiply_fusion
  63.1 1.1 slice_reduce_fusion.7
  64.3 1.7 convolution_multiply_fusion.2
  66.0 1.3 collective-permute-start.1
  67.5 3.4 %collective-permute-done.1 = f32[576,512]{1,0:T(8,128)} collective-permute-done((f32[576,512]{1,0:T(8,128)S(1)}, f32[576,512]{1,0:T(8,128)}, u32[]{:S(2)}, u32[]{:S(2)}) %collective-permute-start.1) | collective-permute-done | bytes 1179680 | tf_op jit(solution)/shard_map/ppermute | solution.py:13
  70.9 0.9 slice.129
  71.8 0.7 convert_element_type.23
  72.5 3.5 %all-to-all-start.1 = ((bf16[16,4,512]{2,1,0:T(4,128)(2,1)}), bf16[16,4,512]{2,1,0:T(4,128)(2,1)S(1)}, u32[]{:S(2)}, u32[]{:S(2)}) async-start(bf16[16,4,512]{2,1,0:T(4,128)(2,1)} %convert_element_type.23), calls=%async_computation.1 | async-start | bytes 131072 | tf_op jit(solution)/shard_map/all_to_all | solution.py:95
  76.0 0.2 reduce-scatter.2.cloned.1.call-start
  76.2 3.4 %fusion.4 = f32[512,1,512]{2,1,0:T(1,128)S(1)} fusion(bf16[4096,512]{1,0:T(8,128)(2,1)} %gather_fusion.1, bf16[512,8,1]{1,0,2:T(8,128)(2,1)S(1)} %get-tuple-element.13), kind=kOutput, calls=%fused_computation.7 | convolution fusion | flops 4194304 | bytes 5251072 | tf_op jit(solution)/shard_map/ik,ikp->ip/dot_general | solution.py:60
  79.6 2.7 all-to-all-done.1
  82.4 0.3 fusion.38
  82.7 2.2 multiply_reduce_fusion
  84.9 0.5 copy-done.4
  85.3 9.5 %convolution_bitcast_fusion = f32[4096,512]{0,1:T(8,128)} fusion(bf16[1,512,4096]{2,1,0:T(8,128)(2,1)S(1)} %copy-done.4, f32[512,512]{1,0:T(8,128)S(1)} %get-tuple-element.30, f32[512]{0:T(512)S(1)} %get-tuple-element.29, f32[512]{0:T(512)S(1)} %add_sqrt_fusion, f32[512,512]{1,0:T(8,128)S(1)} %get-tuple-element.26), kind=kOutput, calls=%fused_computation.4 | convolution fusion | flops 12885950464 | bytes 14684160 | tf_op jit(solution)/shard_map/rd,rp->dp/dot_general | solution.py:107
  94.8 175.8 %reduce-scatter.2.cloned.1.call-done = f32[256,512]{0,1:T(8,128)} async-done(((f32[4096,512]{0,1:T(8,128)}), f32[256,512]{0,1:T(8,128)}) %reduce-scatter.2.cloned.1.call-update) | async-done | bytes 524304 | tf_op jit(solution)/shard_map/reduce_scatter | solution.py:106
  270.7 2.0 copy.18
  (29 shorter events, 1.0 us)
Async XLA Ops:
  18.7 9.0 %copy-start = (s32[512,8]{0,1:T(8,128)S(1)}, s32[512,8]{0,1:T(8,128)}, u32[]{:S(2)}) copy-start(s32[512,8]{0,1:T(8,128)} %param.9) | copy-start | bytes 49156
  20.3 13.8 %all-to-all-start = ((bf16[16,4,512]{2,1,0:T(4,128)(2,1)}), bf16[16,4,512]{2,1,0:T(4,128)(2,1)S(1)}, u32[]{:S(2)}, u32[]{:S(2)}) async-start(bf16[16,4,512]{2,1,0:T(4,128)(2,1)} %reshape.54), calls=%async_computation | async-start | bytes 131072 | tf_op jit(solution)/shard_map/all_to_all | solution.py:31
  34.1 5.6 %collective-permute-start = (bf16[576,512]{1,0:T(8,128)(2,1)S(1)}, bf16[576,512]{1,0:T(8,128)(2,1)S(1)}, u32[]{:S(2)}, u32[]{:S(2)}) collective-permute-start(bf16[576,512]{1,0:T(8,128)(2,1)S(1)} %pad_maximum_fusion.1), channel_id=1, source_target_pairs={{16,0},{17,1},{18,2},{19,3},{20,4},{21,5},{22,6},{23,7},{24,8},{25... | collective-permute-start | bytes 1769480 | tf_op jit(solution)/shard_map/ppermute | solution.py:13
  39.8 21.5 %copy-start.2 = (bf16[576,512]{1,0:T(8,128)(2,1)}, bf16[576,512]{1,0:T(8,128)(2,1)S(1)}, u32[]{:S(2)}) copy-start(bf16[576,512]{1,0:T(8,128)(2,1)S(1)} %collective-permute-done) | copy-start | bytes 1769476
  61.3 0.9 copy-start.3
  65.9 1.4 copy-start.1
  66.0 4.9 %collective-permute-start.1 = (f32[576,512]{1,0:T(8,128)S(1)}, f32[576,512]{1,0:T(8,128)}, u32[]{:S(2)}, u32[]{:S(2)}) collective-permute-start(f32[576,512]{1,0:T(8,128)S(1)} %pad_maximum_fusion), channel_id=1, source_target_pairs={{0,16},{1,17},{2,18},{3,19},{4,20},{5,21},{6,22},{7,23},{8,24},{9,... | collective-permute-start | bytes 3538952 | tf_op jit(solution)/shard_map/ppermute | solution.py:13
  72.5 9.9 %all-to-all-start.1 = ((bf16[16,4,512]{2,1,0:T(4,128)(2,1)}), bf16[16,4,512]{2,1,0:T(4,128)(2,1)S(1)}, u32[]{:S(2)}, u32[]{:S(2)}) async-start(bf16[16,4,512]{2,1,0:T(4,128)(2,1)} %convert_element_type.23), calls=%async_computation.1 | async-start | bytes 131072 | tf_op jit(solution)/shard_map/all_to_all | solution.py:95
  76.0 194.7 %reduce-scatter.2.cloned.1.call-start = ((), (), s32[]{:S(2)}) async-start(), calls=%async_computation.3 | async-start | bytes 8912896 | tf_op jit(solution)/shard_map/reduce_scatter | solution.py:106
  82.7 2.7 copy-start.4
Sparse Core Ops, SparseCore 0:
  94.9 175.6 reduce-scatter.1
where the time goes:
time: 282 us; the launch traced here: 280 us
  waiting for transfers between devices  189 us (67%)
  matrix products  33.4 us (12%)
  local copies, waits for them, and re-layouts  24.5 us (9%)
  starting transfers between devices  16.5 us (6%)
  between operations  13.6 us (5%)
    reduce_scatter x1, waiting for transfers between devices, shards(): lax.psum_scatter(jnp.einsum('rd,rp->dp', hidden_rows, d_embedded, precisi...  176 us
    gather x1, local copies, waits for them, and re-layouts, shards(): mined_rows = pulled[neg_slot]  17.3 us
    dot_general x1, matrix products, shards(): jnp.dot(hidden_rows, weights, precision=lax.Precision.HIGHEST, preferred_...  11.3 us
    dot_general x1, matrix products, shards(): jnp.einsum('rd,rp->dp', hidden_rows, d_embedded, precision=lax.Precision....  9.47 us
    all_to_all x1, starting transfers between devices, shards(): lax.all_to_all(normalized_passages[wanted_rows], 'shard', split_axis=0, c...  7.42 us
    all_to_all x1, waiting for transfers between devices, shards(): lax.all_to_all(normalized_passages[wanted_rows], 'shard', split_axis=0, c...  6.36 us
  transfers between devices with their start and end apart: 5, of which 5 were waited for; matrix products, arithmetic and copies ran while one was open for 1% of the time, Pallas kernels for 0%

commit v1 on v0

v1 whole, which is shorter than its diff:
```python
import functools

import jax
import jax.numpy as jnp
from jax import lax
from jax.experimental import pallas as pl
from jax.experimental.pallas import tpu as pltpu
from jax.sharding import PartitionSpec as P

logit_divisor = 0.05
logit_shift = 20.0
epsilon = 1e-06
code_steps = 128.0
code_range = 32700.0
least_value = 1e-30
MESH = pl.DeviceIdType.MESH
VMEM = pltpu.VMEM


def passed_along(block, axis, distance):
    devices = range(lax.axis_size(axis))
    route = [(i - distance, i) for i in devices if i - distance in devices]
    return lax.ppermute(block, axis, route)


def bit_orders(bits):
    low = list(range(bits))
    if bits < 2:
        return [low] * 4
    first = low
    second = [1, 0] + low[2:]
    return [first, second, first, second]


def reduce_kernel(count, orders, hidden_ref, d_ref, out_ref, *scratch):
    bits = len(orders[0])
    parts = len(orders)
    half = count // 2
    rows, depth = hidden_ref.shape
    width = depth // count
    part = d_ref.shape[1] // parts
    terms, acc, codes = scratch[:3]
    sends = scratch[3 : 3 + bits]
    recvs = scratch[3 + bits : 3 + 2 * bits]
    send_sem, recv_sem = scratch[3 + 2 * bits :]
    tower = lax.axis_index("tower")
    me = lax.axis_index("shard")

    def bit_of(number, b):
        return (number // (1 << b)) % 2

    def partner(b):
        return me + (1 - 2 * bit_of(me, b)) * (1 << b)

    barrier = pltpu.get_barrier_semaphore()
    for b in range(bits):
        pl.semaphore_signal(barrier, inc=1, device_id=(tower, partner(b)), device_id_type=MESH)

    for p in range(parts):
        piece = d_ref[:, p * part : (p + 1) * part].T
        upper = piece.astype(jnp.bfloat16)
        terms[p, :part, :] = upper
        terms[p, part:, :] = (piece - upper.astype(jnp.float32)).astype(jnp.bfloat16)

    def product(p, m, leading):
        order = orders[p]
        block = 0
        for t, b in enumerate(order):
            if t == 0:
                own = (bit_of(me, b) + leading) % 2
            else:
                own = (bit_of(me, b) + bit_of(m, bits - 1 - t)) % 2
            block = block + own * (1 << b)
        columns = pl.ds(pl.multiple_of(block * width, width), width)
        both = jnp.dot(terms[p], hidden_ref[:, columns], preferred_element_type=jnp.float32)
        return both[:part] + both[part:]

    def encode(buffer, p, m, value):
        largest = jnp.maximum(jnp.max(jnp.abs(value), axis=0, keepdims=True), least_value)
        code = jnp.ceil(jnp.log2(largest) * code_steps)
        scaled = value * (jnp.exp2(code * (-1.0 / code_steps)) * code_range)
        whole = jnp.round(scaled).astype(jnp.int32).astype(jnp.int16)
        buffer[p, pl.ds(pl.multiple_of(m * part, part), part), :] = whole
        codes[pl.ds(m, 1), :] = code

    def finish(buffer, p, blocks):
        buffer[p, blocks * part : blocks * part + 16, :] = (
            codes[...].astype(jnp.int32).astype(jnp.int16)
        )

    def copy_of(p, k):
        return pltpu.make_async_remote_copy(
            src_ref=sends[k].at[p],
            dst_ref=recvs[k].at[p],
            send_sem=send_sem.at[p, k],
            recv_sem=recv_sem.at[p, k],
            device_id=(tower, partner(orders[p][k])),
            device_id_type=MESH,
        )

    codes[...] = jnp.zeros_like(codes)
    for p in range(parts):

        def first_half(m, carry):
            encode(sends[0], p, m, product(p, m, 1))
            return carry

        lax.fori_loop(0, half, first_half, 0, unroll=2)
        finish(sends[0], p, half)
        if p == 0:
            pl.semaphore_wait(barrier, bits)
        copy_of(p, 0).start()
    for p in range(parts):

        def second_half(m, carry):
            acc[p, m] = product(p, m, 0)
            return carry

        lax.fori_loop(0, half, second_half, 0, unroll=2)

    for k in range(bits):
        blocks = count >> (k + 1)
        for p in range(parts):
            copy_of(p, k).wait_recv()
            got = recvs[k]
            scales = jnp.exp2(
                got[p, blocks * part : blocks * part + 16, :].astype(jnp.int32).astype(jnp.float32)
                * (1.0 / code_steps)
            ) * (1.0 / code_range)
            codes[...] = scales

            def summed(m):
                coded = got[p, pl.ds(pl.multiple_of(m * part, part), part), :]
                value = coded.astype(jnp.int32).astype(jnp.float32)
                return acc[p, m] + value * codes[pl.ds(m, 1), :]

            if k + 1 < bits:
                left = blocks // 2

                def onward(m, carry):
                    acc[p, left + m] = summed(left + m)
                    return carry

                lax.fori_loop(0, left, onward, 0)

                def kept(m, carry):
                    acc[p, m] = summed(m)
                    return carry

                lax.fori_loop(0, left, kept, 0)
                codes[...] = jnp.zeros_like(codes)

                def coded_again(m, carry):
                    encode(sends[k + 1], p, m, acc[p, left + m])
                    return carry

                lax.fori_loop(0, left, coded_again, 0)
                finish(sends[k + 1], p, left)
                copy_of(p, k + 1).start()
            else:
                out_ref[:, p * part : (p + 1) * part] = summed(0).T
    for k in range(bits):
        for p in range(parts):
            copy_of(p, k).wait_send()


def reduced_product(count, hidden_rows, d_embedded):
    rows, depth = hidden_rows.shape
    columns = d_embedded.shape[1]
    bits = count.bit_length() - 1
    orders = bit_orders(bits)
    parts = len(orders)
    part, width = columns // parts, depth // count
    buffers = [
        VMEM((parts, (count >> (k + 1)) * part + 16, width), jnp.int16) for k in range(bits)
    ]
    return pl.pallas_call(
        functools.partial(reduce_kernel, count, orders),
        out_shape=jax.ShapeDtypeStruct((width, columns), jnp.float32),
        in_specs=[pl.BlockSpec(memory_space=VMEM)] * 2,
        out_specs=pl.BlockSpec(memory_space=VMEM),
        scratch_shapes=[
            VMEM((parts, 2 * part, rows), jnp.bfloat16),
            VMEM((parts, count // 2, part, width), jnp.float32),
            VMEM((16, width), jnp.float32),
        ]
        + buffers
        + buffers
        + [pltpu.SemaphoreType.DMA((parts, bits)), pltpu.SemaphoreType.DMA((parts, bits))],
        compiler_params=pltpu.CompilerParams(
            collective_id=0, has_side_effects=True, vmem_limit_bytes=40 * 1024 * 1024
        ),
        cost_estimate=pl.CostEstimate(
            flops=4 * rows * depth * columns, bytes_accessed=8 * rows * depth, transcendentals=0
        ),
    )(hidden_rows, d_embedded)


def shards(hidden, head, pos_local, requests, neg_slot):
    hidden_rows = hidden[0]
    weights = head[0]
    row_count, depth = hidden_rows.shape
    shard_count = lax.axis_size("shard")
    slot_count = requests.shape[2]
    neg_count = neg_slot.shape[1]
    slot_total = shard_count * slot_count
    embedded = jnp.dot(
        hidden_rows, weights, precision=lax.Precision.HIGHEST, preferred_element_type=jnp.float32
    )
    magnitude = jnp.sqrt(jnp.sum(embedded * embedded, axis=1, keepdims=True) + epsilon)
    unit_rows = embedded / magnitude
    normalized = unit_rows.astype(jnp.bfloat16)
    wanted_rows = requests[:, 0, :]
    flat_wanted = wanted_rows.reshape(-1)
    row_ids = jnp.arange(row_count, dtype=jnp.int32)
    owner_table = (row_ids[:, None] == flat_wanted[None, :]).astype(jnp.bfloat16)
    picked = lax.dot_general(
        owner_table, normalized, (((0,), (0,)), ((), ())), preferred_element_type=jnp.float32
    ).astype(jnp.bfloat16)
    sent_rows = lax.all_to_all(
        picked.reshape(shard_count, slot_count, -1),
        "shard",
        split_axis=0,
        concat_axis=0,
        tiled=True,
    )
    joined_rows = jnp.concatenate([normalized, sent_rows.reshape(slot_total, -1)], axis=0)
    arrived_rows = passed_along(joined_rows, "tower", -1)
    scores = jnp.exp(
        jnp.einsum("ot,bt->ob", normalized, arrived_rows, preferred_element_type=jnp.float32)
        / logit_divisor
        - logit_shift
    )
    slot_ids = jnp.arange(slot_total, dtype=jnp.int32)[None, :]
    slot_uses = jnp.zeros((row_count, slot_total), jnp.float32)
    for column in range(neg_count):
        slot_uses = slot_uses + (neg_slot[:, column : column + 1] == slot_ids).astype(jnp.float32)
    cobatch, mined = scores[:, :row_count], scores[:, row_count:]
    total = jnp.sum(cobatch, axis=1, keepdims=True) + jnp.sum(
        mined * slot_uses, axis=1, keepdims=True
    )
    target = (pos_local[:, None] == row_ids[None, :]).astype(jnp.float32)
    dlog = (cobatch / total - target).astype(jnp.bfloat16)
    slot_weight = slot_uses * lax.reduce_precision(mined / total, 8, 7)
    query_grad = (
        jnp.dot(dlog, arrived_rows[:row_count], preferred_element_type=jnp.float32)
        + jnp.dot(
            slot_weight,
            arrived_rows[row_count:].astype(jnp.float32),
            precision=lax.Precision.HIGHEST,
        )
    ) / logit_divisor
    passage_grad = (
        jnp.einsum("en,er->nr", dlog, normalized, preferred_element_type=jnp.float32)
        / logit_divisor
    )
    slot_grad = (
        jnp.dot(slot_weight.T, normalized.astype(jnp.float32), precision=lax.Precision.HIGHEST)
        / logit_divisor
    )
    joined_grads = jnp.concatenate([passage_grad, slot_grad], axis=0)
    arrived_grads = passed_along(joined_grads, "tower", 1)
    got_inbatch = arrived_grads[:row_count]
    got_slots = arrived_grads[row_count:].reshape(shard_count, slot_count, -1)
    returned_slots = lax.all_to_all(
        got_slots.astype(jnp.bfloat16), "shard", split_axis=0, concat_axis=0, tiled=True
    )
    returned = got_inbatch + jnp.dot(
        owner_table, returned_slots.reshape(slot_total, -1), preferred_element_type=jnp.float32
    )
    is_query = lax.axis_index("tower") == 0
    d_unit = jnp.where(is_query, query_grad, returned)
    d_embedded = (
        d_unit - unit_rows * jnp.sum(unit_rows * d_unit, axis=1, keepdims=True)
    ) / magnitude
    power_of_two = shard_count & (shard_count - 1) == 0 and shard_count > 1
    if power_of_two and (depth // shard_count) % 128 == 0:
        return reduced_product(shard_count, hidden_rows, d_embedded)[None]
    head_grad = lax.psum_scatter(
        jnp.einsum(
            "rd,rp->dp",
            hidden_rows,
            d_embedded,
            precision=lax.Precision.HIGHEST,
            preferred_element_type=jnp.float32,
        ),
        "shard",
        scatter_dimension=0,
        tiled=True,
    )
    return head_grad[None]


def solution(mesh):
    placed = (
        P("tower", "shard", None),
        P("tower", None, None),
        P("shard"),
        P(None, "shard", None),
        P("shard", None),
    )
    return jax.shard_map(
        shards, mesh=mesh, in_specs=placed, out_specs=P("tower", "shard", None), check_vma=False
    )
```

time: 282 us -> 110 us (0.39)
  the two profiles are of different devices: /device:TPU:1 before, /device:TPU:0 now
where the time goes in v1:
time: 110 us
  Pallas kernels  54.1 us (49%)
  matrix products  17 us (15%)
  blocking collectives  15.7 us (14%)
  waiting for transfers between devices  10.4 us (9%)
  starting transfers between devices  7.84 us (7%)
  local copies, waits for them, and re-layouts  2.85 us (3%)
  other arithmetic  1.8 us (2%)
    pallas_call x1, Pallas kernels, reduced_product(): pl.pallas_call(functools.partial(reduce_kernel, count, orders), out_shape...  54.1 us
    all_to_all x1, blocking collectives, shards(): lax.all_to_all(picked.reshape(shard_count, slot_count, -1), 'shard', spli...  15.7 us
    dot_general x1, matrix products, shards(): jnp.dot(hidden_rows, weights, precision=lax.Precision.HIGHEST, preferred_...  11.3 us
    all_to_all x1, waiting for transfers between devices, shards(): lax.all_to_all(got_slots.astype(jnp.bfloat16), 'shard', split_axis=0, con...  6.03 us
    ppermute x2, waiting for transfers between devices, passed_along(): return lax.ppermute(block, axis, route)  4.35 us
    ppermute x2, starting transfers between devices, passed_along(): return lax.ppermute(block, axis, route)  4.34 us
    all_to_all x1, starting transfers between devices, shards(): lax.all_to_all(got_slots.astype(jnp.bfloat16), 'shard', split_axis=0, con...  3.5 us
    dot_general x1, matrix products, shards(): jnp.dot(dlog, arrived_rows[:row_count], preferred_element_type=jnp.float32)  2.23 us
  transfers between devices with their start and end apart: 3, of which 3 were waited for; matrix products, arithmetic and copies ran while one was open for 1% of the time, Pallas kernels for 0%

profile of v1, /device:TPU:0, one launch (start us, length us, event | category | flops | bytes accessed | tf_op | source)
XLA Modules:
  0.0 109.8 jit_solution(12568539800844735389)
XLA Ops:
  0.0 11.3 %multiply_reduce_fusion.1 = (f32[512]{0:T(512)S(1)}, f32[512,512]{1,0:T(8,128)S(1)}) fusion(f32[1,4096,512]{2,1,0:T(8,128)} %param.6, bf16[1,512,4096]{2,1,0:T(8,128)(2,1)} %param.5), kind=kOutput, calls=%fused_computation.17 | convolution fusion | flops 12885426176 | bytes 13633536 | tf_op jit(solution)/shard_map/dot_general | solution.py:207
  11.3 0.0 copy-done.3
  11.3 0.1 copy.10
  11.4 0.1 eq.153
  11.5 0.1 fusion.13
  11.7 0.0 copy-start.1
  11.7 0.2 convolution_convert_fusion
  12.0 15.7 %all_to_all.10 = bf16[16,4,512]{2,1,0:T(4,128)(2,1)S(1)} all-to-all(bf16[16,4,512]{2,1,0:T(4,128)(2,1)S(1)} %reshape.26), channel_id=1, replica_groups=mesh['tower'=2,'shard'=16] {'shard'}, dimensions={0} | all-to-all | bytes 131072 | tf_op jit(solution)/shard_map/all_to_all | solution.py:220
  27.7 1.3 %collective-permute-start = (bf16[576,512]{1,0:T(8,128)(2,1)S(1)}, bf16[576,512]{1,0:T(8,128)(2,1)S(1)}, u32[]{:S(2)}, u32[]{:S(2)}) collective-permute-start(bf16[576,512]{1,0:T(8,128)(2,1)S(1)} %pad_maximum_fusion.1), channel_id=1, source_target_pairs={{16,0},{17,1},{18,2},{19,3},{20,4},{21,5},{22,6},{23,7},{24,8},{25... | collective-permute-start | bytes 1769480 | tf_op jit(solution)/shard_map/ppermute | solution.py:23
  29.0 2.6 %collective-permute-done = bf16[576,512]{1,0:T(8,128)(2,1)S(1)} collective-permute-done((bf16[576,512]{1,0:T(8,128)(2,1)S(1)}, bf16[576,512]{1,0:T(8,128)(2,1)S(1)}, u32[]{:S(2)}, u32[]{:S(2)}) %collective-permute-start) | collective-permute-done | bytes 589856 | tf_op jit(solution)/shard_map/ppermute | solution.py:23
  31.6 0.5 fusion.3
  32.1 0.0 copy-start.4
  32.1 0.1 slice_reduce_fusion
  32.2 0.1 multiply_reduce_fusion.2
  32.4 0.0 copy-done.2
  32.4 0.5 convolution_multiply_fusion.2
  32.9 0.4 convolution_multiply_fusion.1
  33.3 1.1 %pad_maximum_fusion = f32[576,512]{1,0:T(8,128)} fusion(f32[64,512]{1,0:T(8,128)S(1)} %convolution_multiply_fusion.2, f32[512,512]{1,0:T(8,128)S(1)} %convolution_multiply_fusion.1), kind=kLoop, calls=%fused_computation.9 | loop fusion | flops 294912 | bytes 2359296 | tf_op jit(solution)/shard_map/concatenate | solution.py:261
  34.5 3.0 %collective-permute-start.1 = (f32[576,512]{1,0:T(8,128)}, f32[576,512]{1,0:T(8,128)}, u32[]{:S(2)}, u32[]{:S(2)}) collective-permute-start(f32[576,512]{1,0:T(8,128)} %pad_maximum_fusion), channel_id=1, source_target_pairs={{0,16},{1,17},{2,18},{3,19},{4,20},{5,21},{6,22},{7,23},{8,24},{9,... | collective-permute-start | bytes 3538952 | tf_op jit(solution)/shard_map/ppermute | solution.py:23
  37.5 1.8 %collective-permute-done.1 = f32[576,512]{1,0:T(8,128)} collective-permute-done((f32[576,512]{1,0:T(8,128)}, f32[576,512]{1,0:T(8,128)}, u32[]{:S(2)}, u32[]{:S(2)}) %collective-permute-start.1) | collective-permute-done | bytes 1179680 | tf_op jit(solution)/shard_map/ppermute | solution.py:23
  39.3 0.9 slice.79
  40.2 0.7 convert_element_type.55
  40.9 3.5 %all-to-all-start.1 = ((bf16[16,4,512]{2,1,0:T(4,128)(2,1)}), bf16[16,4,512]{2,1,0:T(4,128)(2,1)S(1)}, u32[]{:S(2)}, u32[]{:S(2)}) async-start(bf16[16,4,512]{2,1,0:T(4,128)(2,1)} %convert_element_type.55), calls=%async_computation.1 | async-start | bytes 131072 | tf_op jit(solution)/shard_map/all_to_all | solution.py:265
  44.4 1.5 %fusion.10 = f32[512,512]{1,0:T(8,128)S(1)} fusion(bf16[576,512]{1,0:T(8,128)(2,1)} %copy-done.2, f32[512,576]{0,1:T(8,128)S(1)} %fusion.3, f32[512]{0:T(512)S(1)} %add.56, s32[512]{0:T(512)S(1)} %bitcast.49, s32[512]{0:T(512)S(1)} %bitcast.52, s32[512]{0:T(512)S(1)} %bitcast.34, s32[512]{0:T(512)S(1)} %bitcast.37, s32[512]{0:T(512)S(1)} %bitcast.40, ...), kind=kOutput, calls=%fused_computation.38 | convolution fusion | flops 202178560 | bytes 1263616 | tf_op jit(solution)/shard_map/dot_general | solution.py:247
  45.9 6.0 %all-to-all-done.1 = bf16[16,4,512]{2,1,0:T(4,128)(2,1)S(1)} async-done(((bf16[16,4,512]{2,1,0:T(4,128)(2,1)}), bf16[16,4,512]{2,1,0:T(4,128)(2,1)S(1)}, u32[]{:S(2)}, u32[]{:S(2)}) %all-to-all-start.1) | async-done | bytes 65568 | tf_op jit(solution)/shard_map/all_to_all | solution.py:265
  51.9 0.3 fusion.7
  52.2 0.0 copy-start
  52.2 2.2 %multiply_reduce_fusion = (f32[512]{0:T(512)S(1)}, f32[512,512]{1,0:T(8,128)S(1)}) fusion(f32[512,512]{1,0:T(8,128)S(1)} %get-tuple-element.14, f32[512]{0:T(512)S(1)} %add_sqrt_fusion, f32[512,512]{1,0:T(8,128)S(1)} %fusion.7, f32[576,512]{1,0:T(8,128)} %collective-permute-done.1, f32[512,512]{1,0:T(8,128)S(1)} %fusion.10, bf16[576,512]{1,0:T(8,128)(2,1)} %copy-done.2, ...), kind=kOutput, calls=%fused_computation.14 | convolution fusion | flops 271580672 | bytes 6823937 | tf_op jit(solution)/shard_map/dot_general | solution.py:246
  54.4 0.2 subtract_divide_fusion.d_ref
  54.7 0.2 copy-done
  54.9 54.1 %shard_map.55 = f32[256,512]{1,0:T(8,128)S(1)} custom-call(bf16[512,4096]{1,0:T(8,128)(2,1)S(1)} %bitcast.28, f32[512,512]{1,0:T(8,128)S(1)} %subtract_divide_fusion.d_ref), custom_call_target="tpu_custom_call" | custom-call | flops 4294967296 | bytes 16777216 | tf_op jit(solution)/shard_map/pallas_call | solution.py:177
  109.0 0.8 copy.18
  (11 shorter events, 0.1 us)
Async XLA Ops:
  0.0 11.3 %copy-start.3 = (s32[16,1,4]{0,2,1:T(4,128)S(1)}, s32[16,1,4]{0,2,1:T(4,128)}, u32[]{:S(2)}) copy-start(s32[16,1,4]{0,2,1:T(4,128)} %param.8) | copy-start | bytes 772
  11.7 17.3 %copy-start.1 = (s32[512,8]{0,1:T(8,128)S(1)}, s32[512,8]{0,1:T(8,128)}, u32[]{:S(2)}) copy-start(s32[512,8]{0,1:T(8,128)} %param.9) | copy-start | bytes 49156
  27.7 3.9 %collective-permute-start = (bf16[576,512]{1,0:T(8,128)(2,1)S(1)}, bf16[576,512]{1,0:T(8,128)(2,1)S(1)}, u32[]{:S(2)}, u32[]{:S(2)}) collective-permute-start(bf16[576,512]{1,0:T(8,128)(2,1)S(1)} %pad_maximum_fusion.1), channel_id=1, source_target_pairs={{16,0},{17,1},{18,2},{19,3},{20,4},{21,5},{22,6},{23,7},{24,8},{25... | collective-permute-start | bytes 1769480 | tf_op jit(solution)/shard_map/ppermute | solution.py:23
  31.6 0.8 copy-start.2
  32.1 0.8 copy-start.4
  34.5 4.8 %collective-permute-start.1 = (f32[576,512]{1,0:T(8,128)}, f32[576,512]{1,0:T(8,128)}, u32[]{:S(2)}, u32[]{:S(2)}) collective-permute-start(f32[576,512]{1,0:T(8,128)} %pad_maximum_fusion), channel_id=1, source_target_pairs={{0,16},{1,17},{2,18},{3,19},{4,20},{5,21},{6,22},{7,23},{8,24},{9,... | collective-permute-start | bytes 3538952 | tf_op jit(solution)/shard_map/ppermute | solution.py:23
  40.9 11.0 %all-to-all-start.1 = ((bf16[16,4,512]{2,1,0:T(4,128)(2,1)}), bf16[16,4,512]{2,1,0:T(4,128)(2,1)S(1)}, u32[]{:S(2)}, u32[]{:S(2)}) async-start(bf16[16,4,512]{2,1,0:T(4,128)(2,1)} %convert_element_type.55), calls=%async_computation.1 | async-start | bytes 131072 | tf_op jit(solution)/shard_map/all_to_all | solution.py:265
  52.2 2.7 %copy-start = (bf16[1,512,4096]{2,1,0:T(8,128)(2,1)S(1)}, bf16[1,512,4096]{2,1,0:T(8,128)(2,1)}, u32[]{:S(2)}) copy-start(bf16[1,512,4096]{2,1,0:T(8,128)(2,1)} %param.5) | copy-start | bytes 12582916

commit v2 on v1

--- a/solution.py
+++ b/solution.py
@@ -32,10 +32,211 @@
     return [first, second, first, second]
 
 
-def reduce_kernel(count, orders, hidden_ref, d_ref, out_ref, *scratch):
+def front(
+    count,
+    hidden_hbm,
+    head_hbm,
+    positive_ref,
+    wanted_ref,
+    negative_ref,
+    hidden_ref,
+    head_ref,
+    unit_ref,
+    scale_ref,
+    unit_b_ref,
+    mate_ref,
+    dlog_ref,
+    dlog_got_ref,
+    grad_ref,
+    slots_out_ref,
+    slots_in_ref,
+    load_sem,
+    pair_sem,
+    slot_send_sem,
+    slot_recv_sem,
+    greet,
+):
+    tower = lax.axis_index("tower")
+    me = lax.axis_index("shard")
+    rows, depth = hidden_ref.shape
+    columns = unit_ref.shape[1]
+    chunks = load_sem.shape[1]
+    chunk = depth // chunks
+    slots = count * slots_in_ref.shape[1]
+    lane_groups = columns // 128
+    picks = slots // (count * lane_groups)
+    per_owner = picks * lane_groups
+
+    def loads(c):
+        span = pl.ds(c * chunk, chunk)
+        return (
+            pltpu.make_async_copy(hidden_hbm.at[:, span], hidden_ref.at[:, span], load_sem.at[0, c]),
+            pltpu.make_async_copy(head_hbm.at[span, :], head_ref.at[span, :], load_sem.at[1, c]),
+        )
+
+    def to_mate(source, target, which):
+        return pltpu.make_async_remote_copy(
+            src_ref=source,
+            dst_ref=target,
+            send_sem=pair_sem.at[which],
+            recv_sem=pair_sem.at[which + 1],
+            device_id=(1 - tower, me),
+            device_id_type=MESH,
+        )
+
+    def slot_copy(i):
+        other = lax.rem(me + i, count)
+        return pltpu.make_async_remote_copy(
+            src_ref=slots_out_ref.at[other],
+            dst_ref=slots_in_ref.at[me],
+            send_sem=slot_send_sem.at[i],
+            recv_sem=slot_recv_sem.at[me],
+            device_id=(1 - tower, other),
+            device_id_type=MESH,
+        )
+
+    def slots_arrive():
+        for o in range(count):
+            pltpu.make_async_remote_copy(
+                src_ref=slots_out_ref.at[o],
+                dst_ref=slots_in_ref.at[o],
+                send_sem=slot_send_sem.at[o],
+                recv_sem=slot_recv_sem.at[o],
+                device_id=(1 - tower, me),
+                device_id_type=MESH,
+            ).wait_recv()
+
+    def dot(left, right, dims):
+        return lax.dot_general(left, right, (dims, ((), ())), preferred_element_type=jnp.float32)
+
+    def group_of(shape, axis):
+        return (lax.broadcasted_iota(jnp.int32, shape, axis) >> (picks.bit_length() - 1)) & (
+            lane_groups - 1
+        )
+
+    def send_slots(table):
+        group = group_of((slots, 128), 0)
+        packed = jnp.zeros((slots, 128), jnp.float32)
+        for q in range(lane_groups):
+            packed = packed + jnp.where(group == q, table[:, q * 128 : (q + 1) * 128], 0.0)
+        packed = packed.astype(jnp.bfloat16)
+        for o in range(count):
+            slots_out_ref[o] = packed[o * per_owner : (o + 1) * per_owner, :]
+        for i in range(count):
+            slot_copy(i).start()
+
+    def read_slots():
+        packed = jnp.concatenate([slots_in_ref[o] for o in range(count)], axis=0)
+        row = lax.broadcasted_iota(jnp.int32, (slots, slots), 0)
+        column = lax.broadcasted_iota(jnp.int32, (slots, slots), 1)
+        low, high = picks - 1, -per_owner
+        same = ((row & low) == (column & low)) & ((row & high) == (column & high))
+        group = group_of((slots, slots), 1)
+        pieces = []
+        for q in range(lane_groups):
+            chosen = (same & (group == q)).astype(jnp.float32).astype(jnp.bfloat16)
+            pieces.append(dot(chosen, packed, ((1,), (0,))).astype(jnp.bfloat16))
+        return jnp.concatenate(pieces, axis=1)
+
+    for c in range(chunks):
+        for load in loads(c):
+            load.start()
+    for c in range(chunks):
+        for load in loads(c):
+            load.wait()
+        span = slice(c * chunk, (c + 1) * chunk)
+        weights = head_ref[span, :]
+        first = weights.astype(jnp.bfloat16)
+        left = weights - first.astype(jnp.float32)
+        second = left.astype(jnp.bfloat16)
+        third = (left - second.astype(jnp.float32)).astype(jnp.bfloat16)
+        block = hidden_ref[:, span]
+        term = (
+            dot(block, third, ((1,), (0,)))
+            + dot(block, second, ((1,), (0,)))
+            + dot(block, first, ((1,), (0,)))
+        )
+        if c == 0:
+            unit_ref[...] = term
+        else:
+            unit_ref[...] += term
+    embedded = unit_ref[...]
+    inverse = 1.0 / jnp.sqrt(jnp.sum(embedded * embedded, axis=1, keepdims=True) + epsilon)
+    unit = embedded * inverse
+    unit_ref[...] = unit
+    scale_ref[...] = inverse
+    unit_b_ref[...] = unit.astype(jnp.bfloat16)
+    greet()
+    to_mate(unit_b_ref, mate_ref, 0).start()
+    lane_owner = lax.broadcasted_iota(jnp.int32, (rows, slots), 0) == wanted_ref[...]
+
+    @pl.when(tower == 1)
+    def _():
+        table = lane_owner.astype(jnp.float32).astype(jnp.bfloat16)
+        send_slots(dot(table, unit_b_ref[...], ((0,), (0,))))
+        to_mate(unit_b_ref, mate_ref, 0).wait_recv()
+        to_mate(dlog_ref, dlog_got_ref, 2).wait_recv()
+        grad_ref[...] = dot(dlog_got_ref[...], mate_ref[...], ((0,), (0,))) / logit_divisor
+        slots_arrive()
+        once = lane_owner & (group_of((rows, slots), 1) == 0)
+        grad_ref[...] += dot(
+            once.astype(jnp.float32).astype(jnp.bfloat16), read_slots(), ((1,), (0,))
+        )
+
+    @pl.when(tower == 0)
+    def _():
+        lane = lax.broadcasted_iota(jnp.int32, (rows, slots), 1)
+        slot_id = (lane >> (per_owner.bit_length() - 1)) * picks + (lane & (picks - 1))
+        uses = jnp.zeros((rows, slots), jnp.float32)
+        for k in range(negative_ref.shape[1]):
+            uses = uses + (negative_ref[:, k : k + 1] == slot_id).astype(jnp.float32)
+        once = (group_of((rows, slots), 1) == 0).astype(jnp.float32)
+        to_mate(unit_b_ref, mate_ref, 0).wait_recv()
+        cobatch = jnp.exp(
+            dot(unit_b_ref[...], mate_ref[...], ((1,), (1,))) / logit_divisor - logit_shift
+        )
+        cobatch_sum = jnp.sum(cobatch, axis=1, keepdims=True)
+        slots_arrive()
+        pulled = read_slots()
+        mined = jnp.exp(
+            dot(unit_b_ref[...], pulled, ((1,), (1,))) / logit_divisor - logit_shift
+        )
+        share = 1.0 / (cobatch_sum + jnp.sum(mined * uses * once, axis=1, keepdims=True))
+        target = lax.broadcasted_iota(jnp.int32, (rows, rows), 1) == positive_ref[...]
+        dlog_ref[...] = (cobatch * share - target.astype(jnp.float32)).astype(jnp.bfloat16)
+        to_mate(dlog_ref, dlog_got_ref, 2).start()
+        weight = uses * (mined * share).astype(jnp.bfloat16).astype(jnp.float32)
+        upper = weight.astype(jnp.bfloat16)
+        lower = (weight - upper.astype(jnp.float32)).astype(jnp.bfloat16)
+        slot_grad = dot(upper, unit_b_ref[...], ((0,), (0,))) + dot(
+            lower, unit_b_ref[...], ((0,), (0,))
+        )
+        send_slots(slot_grad / logit_divisor)
+        once_b = once.astype(jnp.bfloat16)
+        grad_ref[...] = (
+            dot(dlog_ref[...], mate_ref[...], ((1,), (0,)))
+            + dot(upper * once_b, pulled, ((1,), (0,)))
+            + dot(lower * once_b, pulled, ((1,), (0,)))
+        ) / logit_divisor
+        to_mate(dlog_ref, dlog_got_ref, 2).wait_send()
+
+    d_unit, unit = grad_ref[...], unit_ref[...]
+    along = jnp.sum(unit * d_unit, axis=1, keepdims=True)
+    grad_ref[...] = (d_unit - unit * along) * scale_ref[...]
+    to_mate(unit_b_ref, mate_ref, 0).wait_send()
+    for i in range(count):
+        slot_copy(i).wait_send()
+
+
+def whole_kernel(
+    count, orders, hidden_hbm, head_hbm, positive_ref, wanted_ref, negative_ref, out_ref, *scratch
+):
     bits = len(orders[0])
     parts = len(orders)
     half = count // 2
+    hidden_ref, grad_ref = scratch[0], scratch[8]
+    front_refs, scratch = scratch[:15], scratch[15:]
+    d_ref = grad_ref
     rows, depth = hidden_ref.shape
     width = depth // count
     part = d_ref.shape[1] // parts
@@ -55,7 +256,13 @@
     barrier = pltpu.get_barrier_semaphore()
     for b in range(bits):
         pl.semaphore_signal(barrier, inc=1, device_id=(tower, partner(b)), device_id_type=MESH)
-
+    for o in range(count):
+        pl.semaphore_signal(barrier, inc=1, device_id=(1 - tower, o), device_id_type=MESH)
+
+    def greet():
+        pl.semaphore_wait(barrier, bits + count)
+
+    front(count, hidden_hbm, head_hbm, positive_ref, wanted_ref, negative_ref, *front_refs, greet)
     for p in range(parts):
         piece = d_ref[:, p * part : (p + 1) * part].T
         upper = piece.astype(jnp.bfloat16)
@@ -107,8 +314,6 @@
 
         lax.fori_loop(0, half, first_half, 0, unroll=2)
         finish(sends[0], p, half)
-        if p == 0:
-            pl.semaphore_wait(barrier, bits)
         copy_of(p, 0).start()
     for p in range(parts):
 
@@ -164,22 +369,40 @@
             copy_of(p, k).wait_send()
 
 
-def reduced_product(count, hidden_rows, d_embedded):
+def whole_gradient(count, hidden_rows, weights, positive, wanted, negative):
     rows, depth = hidden_rows.shape
-    columns = d_embedded.shape[1]
+    columns = weights.shape[1]
+    slots = wanted.shape[1]
     bits = count.bit_length() - 1
     orders = bit_orders(bits)
     parts = len(orders)
+    chunks = 8
     part, width = columns // parts, depth // count
     buffers = [
         VMEM((parts, (count >> (k + 1)) * part + 16, width), jnp.int16) for k in range(bits)
     ]
+    slot_buffer = VMEM((count, slots // count, 128), jnp.bfloat16)
     return pl.pallas_call(
-        functools.partial(reduce_kernel, count, orders),
+        functools.partial(whole_kernel, count, orders),
         out_shape=jax.ShapeDtypeStruct((width, columns), jnp.float32),
-        in_specs=[pl.BlockSpec(memory_space=VMEM)] * 2,
+        in_specs=[pl.BlockSpec(memory_space=pl.ANY)] * 2 + [pl.BlockSpec(memory_space=VMEM)] * 3,
         out_specs=pl.BlockSpec(memory_space=VMEM),
         scratch_shapes=[
+            VMEM((rows, depth), jnp.bfloat16),
+            VMEM((depth, columns), jnp.float32),
+            VMEM((rows, columns), jnp.float32),
+            VMEM((rows, 1), jnp.float32),
+            VMEM((rows, columns), jnp.bfloat16),
+            VMEM((rows, columns), jnp.bfloat16),
+            VMEM((rows, rows), jnp.bfloat16),
+            VMEM((rows, rows), jnp.bfloat16),
+            VMEM((rows, columns), jnp.float32),
+            slot_buffer,
+            slot_buffer,
+            pltpu.SemaphoreType.DMA((2, chunks)),
+            pltpu.SemaphoreType.DMA((4,)),
+            pltpu.SemaphoreType.DMA((count,)),
+            pltpu.SemaphoreType.DMA((count,)),
             VMEM((parts, 2 * part, rows), jnp.bfloat16),
             VMEM((parts, count // 2, part, width), jnp.float32),
             VMEM((16, width), jnp.float32),
@@ -188,12 +411,12 @@
         + buffers
         + [pltpu.SemaphoreType.DMA((parts, bits)), pltpu.SemaphoreType.DMA((parts, bits))],
         compiler_params=pltpu.CompilerParams(
-            collective_id=0, has_side_effects=True, vmem_limit_bytes=40 * 1024 * 1024
+            collective_id=0, has_side_effects=True, vmem_limit_bytes=54 * 1024 * 1024
         ),
         cost_estimate=pl.CostEstimate(
-            flops=4 * rows * depth * columns, bytes_accessed=8 * rows * depth, transcendentals=0
+            flops=10 * rows * depth * columns, bytes_accessed=12 * rows * depth, transcendentals=0
         ),
-    )(hidden_rows, d_embedded)
+    )(hidden_rows, weights, positive, wanted, negative)
 
 
 def shards(hidden, head, pos_local, requests, neg_slot):
@@ -204,6 +427,13 @@
     slot_count = requests.shape[2]
     neg_count = neg_slot.shape[1]
     slot_total = shard_count * slot_count
+    power_of_two = shard_count & (shard_count - 1) == 0 and shard_count > 1
+    lane_groups = weights.shape[1] // 128
+    if power_of_two and (depth // shard_count) % 128 == 0 and slot_count * lane_groups == 16:
+        wanted = jnp.broadcast_to(requests, (shard_count, lane_groups, slot_count))
+        return whole_gradient(
+            shard_count, hidden_rows, weights, pos_local[:, None], wanted.reshape(1, -1), neg_slot
+        )[None]
     embedded = jnp.dot(
         hidden_rows, weights, precision=lax.Precision.HIGHEST, preferred_element_type=jnp.float32
     )
@@ -273,9 +503,6 @@
     d_embedded = (
         d_unit - unit_rows * jnp.sum(unit_rows * d_unit, axis=1, keepdims=True)
     ) / magnitude
-    power_of_two = shard_count & (shard_count - 1) == 0 and shard_count > 1
-    if power_of_two and (depth // shard_count) % 128 == 0:
-        return reduced_product(shard_count, hidden_rows, d_embedded)[None]
     head_grad = lax.psum_scatter(
         jnp.einsum(
             "rd,rp->dp",

time: 110 us -> 84.3 us (0.77)
  the two profiles are of different devices: /device:TPU:0 before, /device:TPU:1 now
where the time goes in v2:
time: 84.3 us; the launch traced here: 84 us
  Pallas kernels  77.6 us (92%)
  local copies, waits for them, and re-layouts  6.41 us (8%)
    pallas_call x1, Pallas kernels, whole_gradient(): pl.pallas_call(functools.partial(whole_kernel, count, orders), out_shape=...  77.6 us
    unnamed x2, local copies, waits for them, and re-layouts  3.42 us

profile of v2, /device:TPU:1, one launch (start us, length us, event | category | flops | bytes accessed | tf_op | source)
XLA Modules:
  0.0 84.0 jit_solution(12630038338713833325)
XLA Ops:
  0.0 0.8 copy.8
  0.8 0.7 reshape.3.wanted_ref
  1.5 1.5 %copy.9.positive_ref = s32[512,1]{1,0:T(8,128)} copy(s32[512,1]{0,1:T(1,128)} %bitcast.6) | data formatting | bytes 4096 | tf_op jit(solution)/shard_map/broadcast_in_dim | solution.py:435
  3.0 1.6 %copy.10.negative_ref = s32[512,8]{1,0:T(8,128)} copy(s32[512,8]{0,1:T(8,128)} %param.9) | data formatting | bytes 32768 | tf_op args[4]
  4.5 77.6 %shard_map.55 = f32[256,512]{1,0:T(8,128)} custom-call(bf16[512,4096]{1,0:T(8,128)(2,1)} %bitcast.9, f32[4096,512]{1,0:T(8,128)} %bitcast.8, s32[512,1]{1,0:T(8,128)} %copy.9.positive_ref, s32[1,256]{1,0:T(1,128)} %reshape.3.wanted_ref, s32[512,8]{1,0:T(8,128)} %copy.10.negative_ref), custom_call_target="tpu_custom_call" | custom-call | flops 10737418240 | bytes 25165824 | tf_op jit(solution)/shard_map/pallas_call | solution.py:385
  82.2 1.9 %copy.12 = f32[1,256,512]{2,1,0:T(8,128)} copy(f32[1,256,512]{2,1,0:T(8,128)} %bitcast.5) | data formatting | bytes 1048576
  (1 shorter events, 0.0 us)

commit v3 on v2

--- a/solution.py
+++ b/solution.py
@@ -12,6 +12,7 @@
 epsilon = 1e-06
 code_steps = 128.0
 code_range = 32700.0
+PIECES, STAGGER, UNROLL = 2, False, 2
 least_value = 1e-30
 MESH = pl.DeviceIdType.MESH
 VMEM = pltpu.VMEM
@@ -23,13 +24,16 @@
     return lax.ppermute(block, axis, route)
 
 
-def bit_orders(bits):
+def part_plan(columns, bits):
     low = list(range(bits))
-    if bits < 2:
-        return [low] * 4
-    first = low
-    second = [1, 0] + low[2:]
-    return [first, second, first, second]
+    if bits < 3:
+        return [(columns // 2, low)] * 2
+    rest = low[3:]
+    orders = ([0, 1, 2] + rest, [1, 2, 0] + rest, [2, 0, 1] + rest)
+    piece = columns // PIECES
+    wide = (piece * 11 // 32 + 15) // 16 * 16
+    sizes = [wide, wide, piece - 2 * wide]
+    return [(size, order) for _ in range(PIECES) for size, order in zip(sizes, orders)]
 
 
 def front(
@@ -228,22 +232,29 @@
         slot_copy(i).wait_send()
 
 
+def row_starts(count, plan):
+    starts, messages, column, row = [], {}, 0, 0
+    for p, (part, order) in enumerate(plan):
+        starts.append(column)
+        column += part
+        for k in range(len(order)):
+            messages[p, k] = row
+            row += (count >> (k + 1)) * part + 16
+    return starts, messages, row
+
+
 def whole_kernel(
-    count, orders, hidden_hbm, head_hbm, positive_ref, wanted_ref, negative_ref, out_ref, *scratch
+    count, plan, hidden_hbm, head_hbm, positive_ref, wanted_ref, negative_ref, out_ref, *scratch
 ):
-    bits = len(orders[0])
-    parts = len(orders)
+    bits = len(plan[0][1])
+    parts = len(plan)
+    starts, messages, _ = row_starts(count, plan)
     half = count // 2
-    hidden_ref, grad_ref = scratch[0], scratch[8]
+    hidden_ref, d_ref = scratch[0], scratch[8]
     front_refs, scratch = scratch[:15], scratch[15:]
-    d_ref = grad_ref
     rows, depth = hidden_ref.shape
     width = depth // count
-    part = d_ref.shape[1] // parts
-    terms, acc, codes = scratch[:3]
-    sends = scratch[3 : 3 + bits]
-    recvs = scratch[3 + bits : 3 + 2 * bits]
-    send_sem, recv_sem = scratch[3 + 2 * bits :]
+    terms, acc, total, codes, scales, sent, got, send_sem, recv_sem = scratch
     tower = lax.axis_index("tower")
     me = lax.axis_index("shard")
 
@@ -263,14 +274,16 @@
         pl.semaphore_wait(barrier, bits + count)
 
     front(count, hidden_hbm, head_hbm, positive_ref, wanted_ref, negative_ref, *front_refs, greet)
-    for p in range(parts):
-        piece = d_ref[:, p * part : (p + 1) * part].T
-        upper = piece.astype(jnp.bfloat16)
-        terms[p, :part, :] = upper
-        terms[p, part:, :] = (piece - upper.astype(jnp.float32)).astype(jnp.bfloat16)
+    turned = d_ref[...].T
+    upper = turned.astype(jnp.bfloat16)
+    lower = (turned - upper.astype(jnp.float32)).astype(jnp.bfloat16)
+    for p, (part, _) in enumerate(plan):
+        start = starts[p]
+        terms[2 * start : 2 * start + part, :] = upper[start : start + part, :]
+        terms[2 * start + part : 2 * (start + part), :] = lower[start : start + part, :]
 
     def product(p, m, leading):
-        order = orders[p]
+        part, order = plan[p]
         block = 0
         for t, b in enumerate(order):
             if t == 0:
@@ -279,93 +292,103 @@
                 own = (bit_of(me, b) + bit_of(m, bits - 1 - t)) % 2
             block = block + own * (1 << b)
         columns = pl.ds(pl.multiple_of(block * width, width), width)
-        both = jnp.dot(terms[p], hidden_ref[:, columns], preferred_element_type=jnp.float32)
+        both = jnp.dot(
+            terms[2 * starts[p] : 2 * (starts[p] + part), :],
+            hidden_ref[:, columns],
+            preferred_element_type=jnp.float32,
+        )
         return both[:part] + both[part:]
 
-    def encode(buffer, p, m, value):
+    def encode(p, k, m, value):
+        part = plan[p][0]
         largest = jnp.maximum(jnp.max(jnp.abs(value), axis=0, keepdims=True), least_value)
         code = jnp.ceil(jnp.log2(largest) * code_steps)
         scaled = value * (jnp.exp2(code * (-1.0 / code_steps)) * code_range)
         whole = jnp.round(scaled).astype(jnp.int32).astype(jnp.int16)
-        buffer[p, pl.ds(pl.multiple_of(m * part, part), part), :] = whole
+        sent[pl.ds(pl.multiple_of(messages[p, k] + m * part, 16), part), :] = whole
         codes[pl.ds(m, 1), :] = code
 
-    def finish(buffer, p, blocks):
-        buffer[p, blocks * part : blocks * part + 16, :] = (
-            codes[...].astype(jnp.int32).astype(jnp.int16)
-        )
-
     def copy_of(p, k):
+        part, order = plan[p]
+        span = pl.ds(messages[p, k], (count >> (k + 1)) * part + 16)
         return pltpu.make_async_remote_copy(
-            src_ref=sends[k].at[p],
-            dst_ref=recvs[k].at[p],
+            src_ref=sent.at[span, :],
+            dst_ref=got.at[span, :],
             send_sem=send_sem.at[p, k],
             recv_sem=recv_sem.at[p, k],
-            device_id=(tower, partner(orders[p][k])),
+            device_id=(tower, partner(order[k])),
             device_id_type=MESH,
         )
+
+    def finish(p, k):
+        end = messages[p, k] + (count >> (k + 1)) * plan[p][0]
+        sent[end : end + 16, :] = codes[...].astype(jnp.int32).astype(jnp.int16)
 
     codes[...] = jnp.zeros_like(codes)
     for p in range(parts):
 
         def first_half(m, carry):
-            encode(sends[0], p, m, product(p, m, 1))
+            encode(p, 0, m, product(p, m, 1))
             return carry
 
-        lax.fori_loop(0, half, first_half, 0, unroll=2)
-        finish(sends[0], p, half)
-        copy_of(p, 0).start()
-    for p in range(parts):
+        lax.fori_loop(0, half, first_half, 0, unroll=UNROLL)
+        finish(p, 0)
+        if not STAGGER or p < parts // PIECES:
+            copy_of(p, 0).start()
+    for p, (part, _) in enumerate(plan):
 
         def second_half(m, carry):
-            acc[p, m] = product(p, m, 0)
+            acc[m, starts[p] : starts[p] + part, :] = product(p, m, 0)
             return carry
 
-        lax.fori_loop(0, half, second_half, 0, unroll=2)
-
-    for k in range(bits):
+        lax.fori_loop(0, half, second_half, 0, unroll=UNROLL)
+    waited = set()
+    if STAGGER:
+        for p in range(parts // PIECES, parts):
+            copy_of(p - parts // PIECES, 0).wait_send()
+            waited.add((p - parts // PIECES, 0))
+            copy_of(p, 0).start()
+
+    steps = [(k, p) for k in range(bits) for p in range(parts)]
+    if STAGGER:
+        lead = parts // PIECES
+        steps = sorted(steps, key=lambda step: (step[0] + step[1] // lead, step[1]))
+    for k, p in steps:
+        part = plan[p][0]
         blocks = count >> (k + 1)
-        for p in range(parts):
-            copy_of(p, k).wait_recv()
-            got = recvs[k]
-            scales = jnp.exp2(
-                got[p, blocks * part : blocks * part + 16, :].astype(jnp.int32).astype(jnp.float32)
-                * (1.0 / code_steps)
-            ) * (1.0 / code_range)
-            codes[...] = scales
-
-            def summed(m):
-                coded = got[p, pl.ds(pl.multiple_of(m * part, part), part), :]
-                value = coded.astype(jnp.int32).astype(jnp.float32)
-                return acc[p, m] + value * codes[pl.ds(m, 1), :]
-
-            if k + 1 < bits:
-                left = blocks // 2
-
-                def onward(m, carry):
-                    acc[p, left + m] = summed(left + m)
-                    return carry
-
-                lax.fori_loop(0, left, onward, 0)
-
-                def kept(m, carry):
-                    acc[p, m] = summed(m)
-                    return carry
-
-                lax.fori_loop(0, left, kept, 0)
-                codes[...] = jnp.zeros_like(codes)
-
-                def coded_again(m, carry):
-                    encode(sends[k + 1], p, m, acc[p, left + m])
-                    return carry
-
-                lax.fori_loop(0, left, coded_again, 0)
-                finish(sends[k + 1], p, left)
-                copy_of(p, k + 1).start()
-            else:
-                out_ref[:, p * part : (p + 1) * part] = summed(0).T
-    for k in range(bits):
-        for p in range(parts):
+        left = blocks // 2
+        own = slice(starts[p], starts[p] + part)
+        copy_of(p, k).wait_recv()
+        end = messages[p, k] + blocks * part
+        scales[...] = jnp.exp2(
+            got[end : end + 16, :].astype(jnp.int32).astype(jnp.float32) * (1.0 / code_steps)
+        ) * (1.0 / code_range)
+
+        def summed(m):
+            coded = got[pl.ds(pl.multiple_of(messages[p, k] + m * part, 16), part), :]
+            value = coded.astype(jnp.int32).astype(jnp.float32)
+            return acc[m, own, :] + value * scales[pl.ds(m, 1), :]
+
+        if k + 1 < bits:
+
+            def onward(m, carry):
+                encode(p, k + 1, m, summed(left + m))
+                return carry
+
+            lax.fori_loop(0, left, onward, 0)
+            finish(p, k + 1)
+            copy_of(p, k + 1).start()
+
+            def kept(m, carry):
+                acc[m, own, :] = summed(m)
+                return carry
+
+            lax.fori_loop(0, left, kept, 0)
+        else:
+            total[own, :] = summed(0)
+    out_ref[...] = total[...].T
+    for k, p in steps:
+        if (p, k) not in waited:
             copy_of(p, k).wait_send()
 
 
@@ -374,16 +397,14 @@
     columns = weights.shape[1]
     slots = wanted.shape[1]
     bits = count.bit_length() - 1
-    orders = bit_orders(bits)
-    parts = len(orders)
+    plan = part_plan(columns, bits)
+    parts = len(plan)
+    message_rows = row_starts(count, plan)[2]
     chunks = 8
-    part, width = columns // parts, depth // count
-    buffers = [
-        VMEM((parts, (count >> (k + 1)) * part + 16, width), jnp.int16) for k in range(bits)
-    ]
+    width = depth // count
     slot_buffer = VMEM((count, slots // count, 128), jnp.bfloat16)
     return pl.pallas_call(
-        functools.partial(whole_kernel, count, orders),
+        functools.partial(whole_kernel, count, plan),
         out_shape=jax.ShapeDtypeStruct((width, columns), jnp.float32),
         in_specs=[pl.BlockSpec(memory_space=pl.ANY)] * 2 + [pl.BlockSpec(memory_space=VMEM)] * 3,
         out_specs=pl.BlockSpec(memory_space=VMEM),
@@ -403,13 +424,16 @@
             pltpu.SemaphoreType.DMA((4,)),
             pltpu.SemaphoreType.DMA((count,)),
             pltpu.SemaphoreType.DMA((count,)),
-            VMEM((parts, 2 * part, rows), jnp.bfloat16),
-            VMEM((parts, count // 2, part, width), jnp.float32),
+            VMEM((2 * columns, rows), jnp.bfloat16),
+            VMEM((count // 2, columns, width), jnp.float32),
+            VMEM((columns, width), jnp.float32),
             VMEM((16, width), jnp.float32),
-        ]
-        + buffers
-        + buffers
-        + [pltpu.SemaphoreType.DMA((parts, bits)), pltpu.SemaphoreType.DMA((parts, bits))],
+            VMEM((16, width), jnp.float32),
+            VMEM((message_rows, width), jnp.int16),
+            VMEM((message_rows, width), jnp.int16),
+            pltpu.SemaphoreType.DMA((parts, bits)),
+            pltpu.SemaphoreType.DMA((parts, bits)),
+        ],
         compiler_params=pltpu.CompilerParams(
             collective_id=0, has_side_effects=True, vmem_limit_bytes=54 * 1024 * 1024
         ),

time: 84.3 us -> 73.8 us (0.88)
  Pallas kernels: 77.6 us -> 67.1 us
    pallas_call x1, Pallas kernels: 77.6 us -> 67.1 us  [whole_gradient(): pl.pallas_call(functools.partial(whole_kernel, count, plan), out_shape=ja...]
where the time goes in v3:
time: 73.8 us; the launch traced here: 73.5 us
  Pallas kernels  67.1 us (91%)
  local copies, waits for them, and re-layouts  6.41 us (9%)
    pallas_call x1, Pallas kernels, whole_gradient(): pl.pallas_call(functools.partial(whole_kernel, count, plan), out_shape=ja...  67.1 us
    unnamed x2, local copies, waits for them, and re-layouts  3.42 us
    broadcast_in_dim x1, local copies, waits for them, and re-layouts, shards(): pos_local[:, None]  1.53 us

profile of v3, /device:TPU:1, one launch (start us, length us, event | category | flops | bytes accessed | tf_op | source)
XLA Modules:
  0.0 73.5 jit_solution(7191443819127068297)
XLA Ops:
  0.0 0.8 %copy.8 = s32[16,4]{1,0:T(8,128)S(1)} copy(s32[16,4]{0,1:T(4,128)} %bitcast.7) | data formatting | bytes 512 | tf_op jit(solution)/shard_map/broadcast_in_dim | solution.py:457
  0.8 0.7 reshape.3.wanted_ref
  1.5 1.5 %copy.9.positive_ref = s32[512,1]{1,0:T(8,128)} copy(s32[512,1]{0,1:T(1,128)} %bitcast.6) | data formatting | bytes 4096 | tf_op jit(solution)/shard_map/broadcast_in_dim | solution.py:459
  3.0 1.6 %copy.10.negative_ref = s32[512,8]{1,0:T(8,128)} copy(s32[512,8]{0,1:T(8,128)} %param.9) | data formatting | bytes 32768 | tf_op args[4]
  4.5 67.1 %shard_map.55 = f32[256,512]{1,0:T(8,128)} custom-call(bf16[512,4096]{1,0:T(8,128)(2,1)} %bitcast.9, f32[4096,512]{1,0:T(8,128)} %bitcast.8, s32[512,1]{1,0:T(8,128)} %copy.9.positive_ref, s32[1,256]{1,0:T(1,128)} %reshape.3.wanted_ref, s32[512,8]{1,0:T(8,128)} %copy.10.negative_ref), custom_call_target="tpu_custom_call" | custom-call | flops 10737418240 | bytes 25165824 | tf_op jit(solution)/shard_map/pallas_call | solution.py:406
  71.7 1.9 %copy.12 = f32[1,256,512]{2,1,0:T(8,128)} copy(f32[1,256,512]{2,1,0:T(8,128)} %bitcast.5) | data formatting | bytes 1048576
  (1 shorter events, 0.0 us)

commit v4 on v3

--- a/solution.py
+++ b/solution.py
@@ -375,7 +375,7 @@
                 encode(p, k + 1, m, summed(left + m))
                 return carry
 
-            lax.fori_loop(0, left, onward, 0)
+            lax.fori_loop(0, left, onward, 0, unroll=min(left, 2))
             finish(p, k + 1)
             copy_of(p, k + 1).start()
 
@@ -383,7 +383,7 @@
                 acc[m, own, :] = summed(m)
                 return carry
 
-            lax.fori_loop(0, left, kept, 0)
+            lax.fori_loop(0, left, kept, 0, unroll=min(left, 2))
         else:
             total[own, :] = summed(0)
     out_ref[...] = total[...].T

time: 73.8 us -> 73.8 us (level)
  no operation moved by 1% of the time
where the time goes in v4:
time: 73.8 us; the launch traced here: 73.5 us
  Pallas kernels  67.1 us (91%)
  local copies, waits for them, and re-layouts  6.41 us (9%)
    pallas_call x1, Pallas kernels, whole_gradient(): pl.pallas_call(functools.partial(whole_kernel, count, plan), out_shape=ja...  67.1 us
    unnamed x2, local copies, waits for them, and re-layouts  3.42 us
    broadcast_in_dim x1, local copies, waits for them, and re-layouts, shards(): pos_local[:, None]  1.53 us

profile of v4, /device:TPU:1, one launch (start us, length us, event | category | flops | bytes accessed | tf_op | source)
XLA Modules:
  0.0 73.5 jit_solution(16260535123159878622)
XLA Ops:
  0.0 0.8 %copy.8 = s32[16,4]{1,0:T(8,128)S(1)} copy(s32[16,4]{0,1:T(4,128)} %bitcast.7) | data formatting | bytes 512 | tf_op jit(solution)/shard_map/broadcast_in_dim | solution.py:457
  0.8 0.7 reshape.3.wanted_ref
  1.5 1.5 %copy.9.positive_ref = s32[512,1]{1,0:T(8,128)} copy(s32[512,1]{0,1:T(1,128)} %bitcast.6) | data formatting | bytes 4096 | tf_op jit(solution)/shard_map/broadcast_in_dim | solution.py:459
  3.0 1.6 %copy.10.negative_ref = s32[512,8]{1,0:T(8,128)} copy(s32[512,8]{0,1:T(8,128)} %param.9) | data formatting | bytes 32768 | tf_op args[4]
  4.5 67.1 %shard_map.55 = f32[256,512]{1,0:T(8,128)} custom-call(bf16[512,4096]{1,0:T(8,128)(2,1)} %bitcast.9, f32[4096,512]{1,0:T(8,128)} %bitcast.8, s32[512,1]{1,0:T(8,128)} %copy.9.positive_ref, s32[1,256]{1,0:T(1,128)} %reshape.3.wanted_ref, s32[512,8]{1,0:T(8,128)} %copy.10.negative_ref), custom_call_target="tpu_custom_call" | custom-call | flops 10737418240 | bytes 25165824 | tf_op jit(solution)/shard_map/pallas_call | solution.py:406
  71.6 1.9 %copy.12 = f32[1,256,512]{2,1,0:T(8,128)} copy(f32[1,256,512]{2,1,0:T(8,128)} %bitcast.5) | data formatting | bytes 1048576
  (1 shorter events, 0.0 us)
